TPU v7x, 512 devices: a whole 4x8x8 slice. The times are simulated.
512 devices in a mesh: section: 4 (over x), seq: 128 (over z, y, core).
Axes of the slice: x: 4, y: 8, z: 8, core: 2. Of those that a mesh axis runs over, the one named last changes fastest.
Arguments:
- hidden: bfloat16 [65536, 4096], P('seq', 'section'), may hold values from -6 to 6
- norm_gain: bfloat16 [4096], P('section'), may hold values from 0.25 to 1.75
- query_weight: bfloat16 [4096, 512], P(None, 'section')
- key_weight: bfloat16 [4096, 128], P('section')
- value_weight: bfloat16 [4096, 128], P('section'), may hold values from -0.5 to 0.5
- output_weight: bfloat16 [512, 4096], P(None, 'section'), may hold values from -0.25 to 0.25
- block_reach: int32 [512], P('seq'), may hold values from 0 to 2
- header_ids: int32 [2], replicated, may hold values from 0 to 511, as said below
Outputs:
- attention_out: bfloat16 [65536, 4096], P('seq', 'section')
Inputs may be any that keep to these rules, and one draw needn't show every extreme that they name: `header_ids`: the 2 indices are distinct block indices, and the last block, 511, is always one of them, at any position.
All inputs are finite; a program needn't handle non-finite values.
Results may differ from a plain program's by a relative error of at most 0.014.
Values may be sent and summed in bfloat16 or wider, within the bound.
No kernel may reach another device: no remote copies, remote signals or barrier semaphores. Data moves between devices by JAX's collectives and lax.ppermute only.
A program may use at most 64 MiB of HBM per device.

v0:
```python
import math
import jax
import jax.numpy as jnp
from jax import lax
from jax.sharding import PartitionSpec as P

BLOCK = 128
REACH = 2
EPSILON = 1e-05
THETA = 500000.0


def merged(value, axis, combine):
    everything = jax.tree.map(lambda part: lax.all_gather(part, axis), value)
    leading = jax.tree.map(lambda part: part[0], everything)

    def lap(k, so_far):
        return combine(so_far, jax.tree.map(lambda part: part[k], everything))

    return lax.fori_loop(1, lax.axis_size(axis), lap, leading)


def padded(cells, sides, width):
    for axis, dim in sides:
        count = lax.axis_size(axis)
        ends = count - 1
        head = lax.slice_in_dim(cells, 0, width, axis=dim)
        tail = lax.slice_in_dim(cells, cells.shape[dim] - width, cells.shape[dim], axis=dim)
        cells = jnp.concatenate(
            [
                lax.ppermute(tail, axis, [(i, (i + 1) % count) for i in range(ends)]),
                cells,
                lax.ppermute(head, axis, [((i + 1) % count, i) for i in range(ends)]),
            ],
            axis=dim,
        )
    return cells


def tables(positions, head_width):
    middle = head_width // 2
    frequency = jnp.exp(
        -(2.0 / head_width) * math.log(THETA) * jnp.arange(middle, dtype=jnp.float32)
    )
    angles = positions.astype(jnp.float32)[:, None] * frequency[None, :]
    angles = jnp.concatenate([angles, angles], axis=1)
    return (jnp.cos(angles), jnp.sin(angles))


def rotate(values, cosine_table, sine_table):
    middle = values.shape[-1] // 2
    turned = jnp.concatenate([-values[..., middle:], values[..., :middle]], axis=-1)
    return values * cosine_table + turned * sine_table


def combine_parts(earlier, later):
    first_max, first_total, first_out = earlier
    second_max, second_total, second_out = later
    overall = jnp.maximum(first_max, second_max)
    first_factor = jnp.exp(first_max - overall)
    second_factor = jnp.exp(second_max - overall)
    return (
        overall,
        first_total * first_factor + second_total * second_factor,
        first_out * first_factor[:, None] + second_out * second_factor[:, None],
    )


def on_device(
    hidden,
    norm_gain,
    query_weight,
    key_weight,
    value_weight,
    output_weight,
    block_reach,
    header_ids,
):
    row_count = hidden.shape[0]
    part_width = hidden.shape[1]
    head_width = key_weight.shape[1]
    local_blocks = row_count // BLOCK
    total_blocks = local_blocks * lax.axis_size("seq")
    seq_place = lax.axis_index("seq")
    floats = hidden.astype(jnp.float32)
    squares = lax.psum(jnp.sum(floats * floats, axis=1), "section")
    scaling = lax.rsqrt(squares / (part_width * lax.axis_size("section")) + EPSILON)
    normed_part = (floats * scaling[:, None] * norm_gain.astype(jnp.float32)[None, :]).astype(
        jnp.bfloat16
    )
    weight_rows = query_weight
    query_sum = jnp.dot(
        lax.all_gather(normed_part, "section", axis=1, tiled=True),
        weight_rows,
        preferred_element_type=jnp.float32,
    )
    key_sum, value_sum = lax.psum(
        (
            jnp.dot(normed_part, key_weight, preferred_element_type=jnp.float32),
            jnp.dot(normed_part, value_weight, preferred_element_type=jnp.float32),
        ),
        "section",
    )
    positions = seq_place * row_count + jnp.arange(row_count, dtype=jnp.int32)
    cosine_table, sine_table = tables(positions, head_width)
    queries = rotate(query_sum, cosine_table, sine_table).astype(jnp.bfloat16)
    keys_here = rotate(key_sum, cosine_table, sine_table).astype(jnp.bfloat16)
    values_here = value_sum.astype(jnp.bfloat16)
    packed = jnp.concatenate([queries, keys_here, values_here], axis=1)
    block_numbers = seq_place * local_blocks + jnp.arange(local_blocks, dtype=jnp.int32)
    select = header_ids[:, None] == block_numbers[None, :]
    shaped = packed.reshape(local_blocks, BLOCK, 3 * head_width)
    picked = jnp.einsum(
        "hb,bre->hre", select.astype(jnp.bfloat16), shaped, preferred_element_type=jnp.float32
    )
    header_pack = lax.psum(picked, "seq").astype(jnp.bfloat16).reshape(-1, 3 * head_width)
    head_queries = header_pack[:, :head_width]
    head_keys = header_pack[:, head_width : 2 * head_width]
    head_values = header_pack[:, 2 * head_width :]
    inverse_root = 1.0 / math.sqrt(head_width)
    far_scores = (
        jnp.einsum("qd,kd->qk", head_queries, keys_here, preferred_element_type=jnp.float32)
        * inverse_root
    )
    far_max = jnp.max(far_scores, axis=1)
    far_weights = jnp.exp(far_scores - far_max[:, None])
    far_total = jnp.sum(far_weights, axis=1)
    far_out = jnp.dot(
        far_weights.astype(jnp.bfloat16), values_here, preferred_element_type=jnp.float32
    )
    merged_max, merged_total, merged_out = merged(
        (far_max, far_total, far_out), "seq", combine_parts
    )
    header_result = merged_out / merged_total[:, None]
    margin_rows = REACH * BLOCK
    stacked = jnp.concatenate([keys_here, values_here], axis=1)
    extended = padded(stacked, (("seq", 0),), margin_rows)
    near_keys = extended[:, :head_width]
    near_values = extended[:, head_width:]
    extent = row_count + 2 * margin_rows
    key_blocks = seq_place * local_blocks - REACH + jnp.arange(extent, dtype=jnp.int32) // BLOCK
    query_blocks = seq_place * local_blocks + jnp.arange(row_count, dtype=jnp.int32) // BLOCK
    limits = jnp.repeat(block_reach, BLOCK)
    key_header = jnp.any(header_ids[:, None] == key_blocks[None, :], axis=0)
    allowed = (key_blocks >= 0)[None, :] & (key_blocks < total_blocks)[None, :]
    allowed = allowed & (jnp.abs(key_blocks[None, :] - query_blocks[:, None]) <= limits[:, None])
    allowed = allowed & jnp.logical_not(key_header)[None, :]
    near_scores = (
        jnp.einsum("qd,kd->qk", queries, near_keys, preferred_element_type=jnp.float32)
        * inverse_root
    )
    near_scores = jnp.where(allowed, near_scores, -jnp.inf)
    head_scores = (
        jnp.einsum("qd,kd->qk", queries, head_keys, preferred_element_type=jnp.float32)
        * inverse_root
    )
    scores = jnp.concatenate([near_scores, head_scores], axis=1)
    row_top = jnp.max(scores, axis=1)
    weights = jnp.exp(scores - row_top[:, None])
    row_sums = jnp.sum(weights, axis=1)
    joined = jnp.concatenate([near_values, head_values], axis=0)
    mixed_out = (
        jnp.dot(weights.astype(jnp.bfloat16), joined, preferred_element_type=jnp.float32)
        / row_sums[:, None]
    )
    header_local = jnp.einsum(
        "hb,hre->bre", select.astype(jnp.float32), header_result.reshape(-1, BLOCK, head_width)
    )
    is_local_header = jnp.any(select, axis=0)
    attended = jnp.where(
        is_local_header[:, None, None],
        header_local,
        mixed_out.reshape(local_blocks, BLOCK, head_width),
    )
    attended = attended.reshape(row_count, head_width).astype(jnp.bfloat16)
    weight_rows = output_weight
    result = jnp.dot(
        lax.all_gather(attended, "section", axis=1, tiled=True),
        weight_rows,
        preferred_element_type=jnp.float32,
    )
    return result.astype(jnp.bfloat16)


def solution(mesh):
    return jax.shard_map(
        on_device,
        mesh=mesh,
        in_specs=(
            P("seq", "section"),
            P("section"),
            P(None, "section"),
            P("section", None),
            P("section", None),
            P(None, "section"),
            P("seq"),
            P(),
        ),
        out_specs=P("seq", "section"),
        check_vma=False,
    )
```

profile of v0, /device:TPU:64, one launch (start us, length us, event | category | flops | bytes accessed | tf_op | source)
XLA Modules:
  0.0 913.6 jit_solution(16988144689448362159)
XLA Ops:
  7.3 1.5 fusion.2
  8.8 10.5 %psum.28 = f32[512]{0:T(512)S(1)} all-reduce(f32[512]{0:T(512)S(1)} %fusion.2), channel_id=1, replica_groups=mesh['section'=4,'seq'=128] {'section'}, use_global_device_ids=true, to_apply=%region_2.0 | all-reduce | flops 512 | bytes 4096 | tf_op jit(solution)/shard_map/psum | solution.py:86
  19.3 1.6 fusion.4
  20.9 1.2 fusion.53
  23.0 1.7 fusion.54
  24.8 17.2 %all-reduce.5 = bf16[512,128]{0,1:T(8,128)(2,1)S(1)} all-reduce(f32[512,128]{0,1:T(8,128)S(1)} %fusion.54), channel_id=1, replica_groups=mesh['section'=4,'seq'=128] {'section'}, use_global_device_ids=true, to_apply=%region_4.0 | all-reduce | flops 65536 | bytes 393216 | tf_op jit(solution)/shard_map/psum | solution.py:97
  42.0 34.5 %all-reduce.4.cloned.1.call-done = f32[512,128]{0,1:T(8,128)} async-done(((f32[512,128]{0,1:T(8,128)}), f32[512,128]{0,1:T(8,128)}) %all-reduce.4.cloned.1.call-update) | async-done | bytes 262160 | tf_op jit(solution)/shard_map/psum | solution.py:97
  77.5 55.5 %all-gather.8.cloned.1.call-done = bf16[512,4096]{1,0:T(8,128)(2,1)} async-done(((bf16[512,1024]{1,0:T(8,128)(2,1)}), bf16[512,4096]{1,0:T(8,128)(2,1)}) %all-gather.8.cloned.1.call-update) | async-done | bytes 4194320 | tf_op jit(solution)/shard_map/all_gather | solution.py:93
  133.0 3.7 fusion.52
  138.7 461.0 %all-reduce.6 = bf16[2,128,384]{2,0,1:T(2,128)(2,1)S(1)} all-reduce(f32[2,128,384]{2,0,1:T(2,128)S(1)} %fusion.48), channel_id=1, replica_groups=mesh['section'=4,'seq'=128] {'seq'}, use_global_device_ids=true, to_apply=%region_5.0 | all-reduce | flops 98304 | bytes 589824 | tf_op jit(solution)/shard_map/psum | solution.py:116
  601.6 82.4 %all-gather.3 = f32[128,1,256]{2,1,0:T(1,128)S(1)} all-gather(f32[1,1,256]{2,1,0:T(1,128)S(1)} %bitcast.66), channel_id=2, replica_groups=mesh['section'=4,'seq'=128] {'seq'}, dimensions={0}, use_global_device_ids=true | all-gather | bytes 132096 | tf_op jit(solution)/shard_map/all_gather | solution.py:14
  684.3 47.1 %all-gather.4 = f32[128,1,256]{2,1,0:T(1,128)S(1)} all-gather(f32[1,1,256]{2,1,0:T(1,128)S(1)} %bitcast.67), channel_id=3, replica_groups=mesh['section'=4,'seq'=128] {'seq'}, dimensions={0}, use_global_device_ids=true | all-gather | bytes 132096 | tf_op jit(solution)/shard_map/all_gather | solution.py:14
  731.4 4.6 collective-permute-start.1
  736.0 1.9 collective-permute-start
  738.5 5.9 collective-permute-done
  748.1 144.2 %while.19 = (s32[]{:T(128)}, f32[256]{0:T(256)S(1)}, f32[256]{0:T(256)S(1)}, f32[256,128]{1,0:T(8,128)S(1)}, f32[128,256]{1,0:T(8,128)S(1)}, /*index=5*/f32[128,...) while((s32[]{:T(128)}, f32[256]{0:T(256)S(1)}, f32[256]{0:T(256)S(1)}, ...), condition=%wide.region_9.10_spmd, body=%wide.region_8.0_spmd.sunk | while | flops 99845 | bytes 407703 | solution.py:20
  749.3 1.1 fusion.69
  751.5 1.1 fusion.69
  753.8 1.1 fusion.69
  754.9 1.1 fusion.69
  756.1 1.1 fusion.69
  757.2 1.1 fusion.69
  758.3 1.1 fusion.69
  759.5 1.1 fusion.69
  761.7 1.1 fusion.69
  764.0 1.1 fusion.69
  766.3 1.1 fusion.69
  768.6 1.1 fusion.69
  770.8 1.1 fusion.69
  773.1 1.1 fusion.69
  892.8 12.6 %all_gather.31 = bf16[512,512]{1,0:T(8,128)(2,1)S(1)} all-gather(bf16[512,128]{1,0:T(8,128)(2,1)S(1)} %bitcast.59), channel_id=1, replica_groups=mesh['section'=4,'seq'=128] {'section'}, dimensions={1}, use_global_device_ids=true | all-gather | bytes 655360 | tf_op jit(solution)/shard_map/all_gather | solution.py:178
  905.4 1.7 convolution_convert_fusion
  (442 shorter events, 136.4 us)
Async XLA Ops:
  6.5 898.9 %copy-start = (bf16[512,1024]{1,0:T(8,128)(2,1)S(1)}, bf16[512,1024]{1,0:T(8,128)(2,1)}, u32[]{:S(2)}) copy-start(bf16[512,1024]{1,0:T(8,128)(2,1)} %param.15) | copy-start | bytes 3145732
  6.5 14.4 %copy-start.7 = (bf16[1024,128]{1,0:T(8,128)(2,1)S(1)}, bf16[1024,128]{1,0:T(8,128)(2,1)}, u32[]{:S(2)}) copy-start(bf16[1024,128]{1,0:T(8,128)(2,1)} %param.13) | copy-start | bytes 786436
  6.5 70.0 %all-reduce.4.cloned.1.call-start = ((), (), s32[]{:S(2)}) async-start(), calls=%async_computation.1 | async-start | bytes 524288 | tf_op jit(solution)/shard_map/psum | solution.py:97
  19.3 3.6 copy-start.8
  20.9 1.3 copy-start.1
  22.1 110.9 %copy-start.4 = (bf16[4096,128]{1,0:T(8,128)(2,1)S(1)}, bf16[4096,128]{1,0:T(8,128)(2,1)}, u32[]{:S(2)}) copy-start(bf16[4096,128]{1,0:T(8,128)(2,1)} %param.12) | copy-start | bytes 3145732
  22.2 110.8 %all-gather.8.cloned.1.call-start = ((), (), s32[]{:S(2)}) async-start(), calls=%async_computation | async-start | bytes 5242880 | tf_op jit(solution)/shard_map/all_gather | solution.py:93
  22.9 724.2 %all-gather.10.cloned.1.call-start = ((), (), s32[]{:S(2)}) async-start(), calls=%async_computation.2 | async-start | bytes 16908288 | tf_op jit(solution)/shard_map/all_gather | solution.py:14
  77.5 59.2 %copy-start.3 = (f32[512,128]{0,1:T(8,128)S(1)}, f32[512,128]{0,1:T(8,128)}, u32[]{:S(2)}) copy-start(f32[512,128]{0,1:T(8,128)} %all-reduce.4.cloned.1.call-done) | copy-start | bytes 786436
  136.7 1.6 copy-start.9
  138.3 463.3 %copy-start.10 = (s32[4]{0:T(128)S(1)}, s32[4]{0:T(128)}, u32[]{:S(2)}) copy-start(s32[4]{0:T(128)} %param.16) | copy-start | bytes 52
  684.1 61.5 %copy-start.6 = (f32[128,1,256]{2,1,0:T(1,128)}, f32[128,1,256]{2,1,0:T(1,128)S(1)}, u32[]{:S(2)}) copy-start(f32[128,1,256]{2,1,0:T(1,128)S(1)} %all-gather.3) | copy-start | bytes 393220
  731.4 14.1 %copy-start.5 = (f32[128,1,256]{2,1,0:T(1,128)}, f32[128,1,256]{2,1,0:T(1,128)S(1)}, u32[]{:S(2)}) copy-start(f32[128,1,256]{2,1,0:T(1,128)S(1)} %all-gather.4) | copy-start | bytes 393220
  731.4 7.1 collective-permute-start.1
  736.0 8.4 collective-permute-start
  744.5 1.1 copy-start.2
  745.6 1.0 slice-start
  746.5 1.5 slice-start.1
  746.5 1.5 slice-start.2
Sparse Core Ops, SparseCore 0:
  22.3 54.2 all-reduce.3
  78.9 54.1 all-gather.7
  601.4 126.7 all-gather.9
where the time goes:
time: 916 us; the launch traced here: 914 us
  blocking collectives  631 us (69%)
  other arithmetic  146 us (16%)
  waiting for transfers between devices  96.8 us (11%)
  between operations  13.5 us (1%)
  matrix products  12.3 us (1%)
    psum x1, blocking collectives, on_device(): lax.psum(picked, 'seq').astype(jnp.bfloat16).reshape(-1, 3 * head_width)  461 us
    add x127, other arithmetic, combine_parts(): first_out * first_factor[:, None] + second_out * second_factor[:, None]  136 us
    all_gather x2, blocking collectives, merged(): everything = jax.tree.map(lambda part: lax.all_gather(part, axis), value)  130 us
    all_gather x1, waiting for transfers between devices, on_device(): lax.all_gather(normed_part, 'section', axis=1, tiled=True)  55.5 us
    psum x1, waiting for transfers between devices, on_device(): lax.psum((jnp.dot(normed_part, key_weight, preferred_element_type=jnp.flo...  34.5 us
  transfers between devices with their start and end apart: 5, of which 4 were waited for; matrix products, arithmetic and copies ran while one was open for 1% of the time, Pallas kernels for 0%

commit v1 on v0

--- a/solution.py
+++ b/solution.py
@@ -113,7 +113,11 @@
     picked = jnp.einsum(
         "hb,bre->hre", select.astype(jnp.bfloat16), shaped, preferred_element_type=jnp.float32
     )
-    header_pack = lax.psum(picked, "seq").astype(jnp.bfloat16).reshape(-1, 3 * head_width)
+    header_pack = (
+        jnp.sum(lax.all_gather(picked, "seq"), axis=0)
+        .astype(jnp.bfloat16)
+        .reshape(-1, 3 * head_width)
+    )
     head_queries = header_pack[:, :head_width]
     head_keys = header_pack[:, head_width : 2 * head_width]
     head_values = header_pack[:, 2 * head_width :]

time: 916 us -> 625 us (0.68)
  blocking collectives: 631 us -> 142 us
  waiting for transfers between devices: 96.8 us -> 275 us
  other arithmetic: 146 us -> 163 us
    psum x1 -> x0, blocking collectives: 461 us -> none  [on_device(): lax.psum(picked, 'seq').astype(jnp.bfloat16).reshape(-1, 3 * head_width)]
    all_gather x0 -> x1, waiting for transfers between devices: none -> 182 us  [on_device(): lax.all_gather(picked, 'seq')]
    all_gather x2, blocking collectives: 130 us -> 100 us  [merged(): everything = jax.tree.map(lambda part: lax.all_gather(part, axis), value)]
    reduce_sum x0 -> x1, other arithmetic: none -> 17.6 us  [on_device(): jnp.sum(lax.all_gather(picked, 'seq'), axis=0).astype(jnp.bfloat16)]
  transfers between devices with their start and end apart: 5 -> 6, of which waited for: 4 -> 5; matrix products, arithmetic and copies ran while one was open for 1% -> 1% of each run, Pallas kernels for 0% -> 0%
where the time goes in v1:
time: 625 us; the launch traced here: 622 us
  waiting for transfers between devices  275 us (44%)
  other arithmetic  163 us (26%)
  blocking collectives  142 us (23%)
  between operations  13.5 us (2%)
  matrix products  12.3 us (2%)
  starting transfers between devices  8.09 us (1%)
    all_gather x1, waiting for transfers between devices, on_device(): lax.all_gather(picked, 'seq')  182 us
    add x127, other arithmetic, combine_parts(): first_out * first_factor[:, None] + second_out * second_factor[:, None]  136 us
    all_gather x2, blocking collectives, merged(): everything = jax.tree.map(lambda part: lax.all_gather(part, axis), value)  100 us
    all_gather x1, waiting for transfers between devices, on_device(): lax.all_gather(normed_part, 'section', axis=1, tiled=True)  55.5 us
    psum x1, waiting for transfers between devices, on_device(): lax.psum((jnp.dot(normed_part, key_weight, preferred_element_type=jnp.flo...  34.5 us
    reduce_sum x1, other arithmetic, on_device(): jnp.sum(lax.all_gather(picked, 'seq'), axis=0).astype(jnp.bfloat16)  17.6 us
    psum x1, blocking collectives, on_device(): lax.psum((jnp.dot(normed_part, key_weight, preferred_element_type=jnp.flo...  17.2 us
    all_gather x1, blocking collectives, on_device(): lax.all_gather(attended, 'section', axis=1, tiled=True)  14.5 us
  transfers between devices with their start and end apart: 6, of which 5 were waited for; matrix products, arithmetic and copies ran while one was open for 1% of the time, Pallas kernels for 0%

profile of v1, /device:TPU:64, one launch (start us, length us, event | category | flops | bytes accessed | tf_op | source)
XLA Modules:
  0.0 622.4 jit_solution(1750948196864686670)
XLA Ops:
  6.5 1.6 fusion.2
  8.1 10.5 %psum.21 = f32[512]{0:T(512)S(1)} all-reduce(f32[512]{0:T(512)S(1)} %fusion.2), channel_id=1, replica_groups=mesh['section'=4,'seq'=128] {'section'}, use_global_device_ids=true, to_apply=%region_2.0 | all-reduce | flops 512 | bytes 4096 | tf_op jit(solution)/shard_map/psum | solution.py:86
  19.3 1.6 fusion.4
  20.9 1.2 fusion.53
  23.0 1.7 fusion.54
  24.8 17.2 %all-reduce.4 = bf16[512,128]{0,1:T(8,128)(2,1)S(1)} all-reduce(f32[512,128]{0,1:T(8,128)S(1)} %fusion.54), channel_id=1, replica_groups=mesh['section'=4,'seq'=128] {'section'}, use_global_device_ids=true, to_apply=%region_4.0 | all-reduce | flops 65536 | bytes 393216 | tf_op jit(solution)/shard_map/psum | solution.py:97
  42.0 34.5 %all-reduce.3.cloned.1.call-done = f32[512,128]{0,1:T(8,128)} async-done(((f32[512,128]{0,1:T(8,128)}), f32[512,128]{0,1:T(8,128)}) %all-reduce.3.cloned.1.call-update) | async-done | bytes 262160 | tf_op jit(solution)/shard_map/psum | solution.py:97
  77.5 55.5 %all-gather.10.cloned.1.call-done = bf16[512,4096]{1,0:T(8,128)(2,1)} async-done(((bf16[512,1024]{1,0:T(8,128)(2,1)}), bf16[512,4096]{1,0:T(8,128)(2,1)}) %all-gather.10.cloned.1.call-update) | async-done | bytes 4194320 | tf_op jit(solution)/shard_map/all_gather | solution.py:93
  133.0 3.7 fusion.52
  139.5 181.7 %all-gather.12.cloned.1.call-done = f32[256,128,384]{2,1,0:T(8,128)} async-done(((f32[2,128,384]{2,1,0:T(8,128)}), f32[256,128,384]{2,1,0:T(8,128)}) %all-gather.12.cloned.1.call-update) | async-done | bytes 50331664 | tf_op jit(solution)/shard_map/all_gather | solution.py:117
  321.2 17.6 %reduce_sum.37 = bf16[2,128,384]{2,1,0:T(8,128)(2,1)S(1)} reduce(f32[128,2,128,384]{3,2,1,0:T(8,128)} %bitcast.54, f32[]{:T(128)} %constant.86.clone.1), dimensions={0}, to_apply=%region_5.0 | reduce | flops 12484608 | bytes 50528260 | tf_op jit(solution)/shard_map/reduce_sum | solution.py:117
  340.5 2.2 collective-permute-start
  342.7 5.8 collective-permute-start.1
  349.2 1.8 collective-permute-done.1
  352.4 50.4 %all-gather.5 = f32[128,1,256]{2,1,0:T(1,128)S(1)} all-gather(f32[1,1,256]{2,1,0:T(1,128)S(1)} %bitcast.69), channel_id=4, replica_groups=mesh['section'=4,'seq'=128] {'seq'}, dimensions={0}, use_global_device_ids=true | all-gather | bytes 132096 | tf_op jit(solution)/shard_map/all_gather | solution.py:14
  402.9 49.6 %all-gather.4 = f32[128,1,256]{2,1,0:T(1,128)S(1)} all-gather(f32[1,1,256]{2,1,0:T(1,128)S(1)} %bitcast.68), channel_id=3, replica_groups=mesh['section'=4,'seq'=128] {'seq'}, dimensions={0}, use_global_device_ids=true | all-gather | bytes 132096 | tf_op jit(solution)/shard_map/all_gather | solution.py:14
  455.0 144.2 %while.19 = (s32[]{:T(128)}, f32[256]{0:T(256)S(1)}, f32[256]{0:T(256)S(1)}, f32[256,128]{1,0:T(8,128)S(1)}, f32[128,256]{1,0:T(8,128)S(1)}, /*index=5*/f32[128,...) while((s32[]{:T(128)}, f32[256]{0:T(256)S(1)}, f32[256]{0:T(256)S(1)}, ...), condition=%wide.region_9.10_spmd, body=%wide.region_8.0_spmd.sunk | while | flops 99845 | bytes 407703 | solution.py:20
  455.0 1.1 fusion.69
  457.3 1.1 fusion.69
  458.4 1.1 fusion.69
  459.6 1.1 fusion.69
  460.7 1.1 fusion.69
  461.8 1.1 fusion.69
  463.0 1.1 fusion.69
  465.2 1.1 fusion.69
  467.5 1.1 fusion.69
  469.8 1.1 fusion.69
  472.1 1.1 fusion.69
  474.3 1.1 fusion.69
  476.6 1.1 fusion.69
  599.7 14.5 %all_gather.39 = bf16[512,512]{1,0:T(8,128)(2,1)S(1)} all-gather(bf16[512,128]{1,0:T(8,128)(2,1)S(1)} %bitcast.59), channel_id=1, replica_groups=mesh['section'=4,'seq'=128] {'section'}, dimensions={1}, use_global_device_ids=true | all-gather | bytes 655360 | tf_op jit(solution)/shard_map/all_gather | solution.py:182
  614.2 1.7 convolution_convert_fusion
  (440 shorter events, 138.2 us)
Async XLA Ops:
  6.5 607.6 %copy-start = (bf16[512,1024]{1,0:T(8,128)(2,1)S(1)}, bf16[512,1024]{1,0:T(8,128)(2,1)}, u32[]{:S(2)}) copy-start(bf16[512,1024]{1,0:T(8,128)(2,1)} %param.15) | copy-start | bytes 3145732
  6.5 14.4 %copy-start.5 = (bf16[1024,128]{1,0:T(8,128)(2,1)S(1)}, bf16[1024,128]{1,0:T(8,128)(2,1)}, u32[]{:S(2)}) copy-start(bf16[1024,128]{1,0:T(8,128)(2,1)} %param.13) | copy-start | bytes 786436
  6.5 70.0 %all-reduce.3.cloned.1.call-start = ((), (), s32[]{:S(2)}) async-start(), calls=%async_computation.1 | async-start | bytes 524288 | tf_op jit(solution)/shard_map/psum | solution.py:97
  19.3 3.6 copy-start.6
  20.9 1.3 copy-start.1
  22.1 110.9 %copy-start.4 = (bf16[4096,128]{1,0:T(8,128)(2,1)S(1)}, bf16[4096,128]{1,0:T(8,128)(2,1)}, u32[]{:S(2)}) copy-start(bf16[4096,128]{1,0:T(8,128)(2,1)} %param.12) | copy-start | bytes 3145732
  22.1 110.8 %all-gather.10.cloned.1.call-start = ((), (), s32[]{:S(2)}) async-start(), calls=%async_computation | async-start | bytes 5242880 | tf_op jit(solution)/shard_map/all_gather | solution.py:93
  22.9 298.3 %all-gather.12.cloned.1.call-start = ((), (), s32[]{:S(2)}) async-start(), calls=%async_computation.2 | async-start | bytes 50724864 | tf_op jit(solution)/shard_map/all_gather | solution.py:117
  77.5 59.2 %copy-start.3 = (f32[512,128]{0,1:T(8,128)S(1)}, f32[512,128]{0,1:T(8,128)}, u32[]{:S(2)}) copy-start(f32[512,128]{0,1:T(8,128)} %all-reduce.3.cloned.1.call-done) | copy-start | bytes 786436
  136.7 1.6 copy-start.7
  139.5 314.6 %all-gather.14.cloned.1.call-start = ((), (), s32[]{:S(2)}) async-start(), calls=%async_computation.3 | async-start | bytes 16908288 | tf_op jit(solution)/shard_map/all_gather | solution.py:14
  338.8 1.6 copy-start.8
  340.5 8.7 %collective-permute-start = (bf16[256,256]{0,1:T(8,128)(2,1)S(1)}, bf16[256,256]{0,1:T(8,128)(2,1)S(1)}, u32[]{:S(2)}, u32[]{:S(2)}) collective-permute-start(bf16[256,256]{0,1:T(8,128)(2,1)S(1)} %get-tuple-element.204), channel_id=1, source_target_pairs={{0,1},{1,2},{2,3},{3,4},{4,5},{5,6},{6,7},{7,8},{8,9},{9,10},{10,1... | collective-permute-start | bytes 393224 | tf_op jit(solution)/shard_map/ppermute | solution.py:31
  342.7 8.3 %collective-permute-start.1 = (bf16[256,256]{0,1:T(8,128)(2,1)S(1)}, bf16[256,256]{0,1:T(8,128)(2,1)S(1)}, u32[]{:S(2)}, u32[]{:S(2)}) collective-permute-start(bf16[256,256]{0,1:T(8,128)(2,1)S(1)} %get-tuple-element.205), channel_id=1, source_target_pairs={{1,0},{2,1},{3,2},{4,3},{5,4},{6,5},{7,6},{8,7},{9,8},{10,9},{11,1... | collective-permute-start | bytes 393224 | tf_op jit(solution)/shard_map/ppermute | solution.py:33
  351.1 1.1 copy-start.2
  402.8 50.6 %slice-start = ((bf16[1024,256]{0,1:T(8,128)(2,1)}), bf16[1024,128]{0,1:T(8,128)(2,1)S(1)}, s32[]{:S(2)}) async-start(bf16[1024,256]{0,1:T(8,128)(2,1)} %copy-done.2), calls=%async_computation.4 | async-start | bytes 524288 | tf_op jit(solution)/shard_map/slice | solution.py:143
Sparse Core Ops, SparseCore 0:
  22.3 54.2 all-reduce.2
  78.8 54.1 all-gather.9
  139.6 181.5 all-gather.11
  340.4 98.8 all-gather.13
